TPU v7x, 32 devices: a whole 2x2x4 slice. The times are simulated.
32 devices in a mesh: row: 4 (over y, x), col: 8 (over z, core).
Axes of the slice: x: 2, y: 2, z: 4, core: 2. Of those that a mesh axis runs over, the one named last changes fastest.
Arguments:
- user_emb: bfloat16 [8192, 256], P(('row', 'col')), may hold values from -8 to 8
- item_emb: bfloat16 [8192, 256], P(('row', 'col')), may hold values from -8 to 8
- user_cot: bfloat16 [8192, 256], P(('row', 'col')), may hold values from -8 to 8
- item_cot: bfloat16 [8192, 256], P(('row', 'col')), may hold values from -8 to 8
- tiles: bfloat16 [8192, 5120], P('row', 'col'), may hold values from 0 to 1, as said below
- tile_cols: int32 [64, 40], P('row', 'col'), may hold values from 0 to 7, as said below
- row_count: int32 [64, 8], P('row', 'col'), may hold values from 1 to 5, as said below
- user_deg: int32 [8192], P(('row', 'col')), may hold values from 6 to 21
- item_deg: int32 [8192], P(('row', 'col')), may hold values from 6 to 21
Outputs:
- user_next: float32 [8192, 256], P(('row', 'col'))
- item_next: float32 [8192, 256], P(('row', 'col'))
- user_grad: float32 [8192, 256], P(('row', 'col'))
- item_grad: float32 [8192, 256], P(('row', 'col'))
Inputs may be any that keep to these rules, and one draw needn't show every extreme that they name: `tiles`: every entry is 0 or 1. `tile_cols`: within one block row of one device, the 5 slots name distinct item blocks; slots at or beyond row_count are unused. `row_count`: in every draw some block row of some device holds 5 tiles.
All inputs are finite; a program needn't handle non-finite values.
Results may differ from a plain program's by a relative error of at most 0.0029.
Values may be sent and summed in bfloat16 or wider, within the bound.
No kernel may reach another device: no remote copies, remote signals or barrier semaphores. Data moves between devices by JAX's collectives and lax.ppermute only.
A program may use at most 128 MiB of HBM per device.

v0:
```python
import math

import jax
import jax.numpy as jnp
from jax import lax
from jax.sharding import PartitionSpec as P


def scaled_side(former, latter, inverse_root):
    joined = jnp.concatenate([former, latter], axis=1).astype(jnp.float32)
    return (joined * inverse_root[:, None]).astype(jnp.bfloat16)


def spread_rows(tile_group, col_group, item_blocks):
    selector = (
        col_group[:, :, None] == jnp.arange(item_blocks, dtype=jnp.int32)[None, None, :]
    ).astype(jnp.bfloat16)
    return jnp.einsum("gikj,gkc->gicj", tile_group, selector)


def row_products(dense_rows, item_grid):
    return jnp.einsum("gicj,cjf->gif", dense_rows, item_grid, preferred_element_type=jnp.float32)


def column_products(dense_rows, user_group):
    return jnp.einsum("gicj,gif->cjf", dense_rows, user_group, preferred_element_type=jnp.float32)


def padded_pass(tile_grid, live_cols, user_blocks, item_grid):
    block_rows, block_size, slot_count, _ = tile_grid.shape
    doubled = user_blocks.shape[-1]
    item_blocks = item_grid.shape[0]
    group_size = math.gcd(block_rows, 8)
    turn_count = block_rows // group_size
    tile_groups = tile_grid.reshape(turn_count, group_size, block_size, slot_count, block_size)
    col_groups = live_cols.reshape(turn_count, group_size, slot_count)
    user_groups = user_blocks.reshape(turn_count, group_size, block_size, doubled)

    def advance(item_sum, pieces):
        tile_group, col_group, user_group = pieces
        dense_rows = spread_rows(tile_group, col_group, item_blocks)
        item_sum = item_sum + column_products(dense_rows, user_group)
        return (item_sum, row_products(dense_rows, item_grid))

    start_sum = jnp.zeros((item_blocks, block_size, doubled), jnp.float32)
    item_sum, user_parts = lax.scan(advance, start_sum, (tile_groups, col_groups, user_groups))
    user_partial = user_parts.reshape(block_rows * block_size, doubled)
    return (user_partial, item_sum.reshape(item_blocks * block_size, doubled))


def shards(user_emb, item_emb, user_cot, item_cot, tiles, tile_cols, row_count, user_deg, item_deg):
    width = user_emb.shape[1]
    doubled = 2 * width
    block_rows, slot_count = tile_cols.shape
    block_size = tiles.shape[0] // block_rows
    user_root = 1.0 / jnp.sqrt(user_deg.astype(jnp.float32))
    item_root = 1.0 / jnp.sqrt(item_deg.astype(jnp.float32))
    user_side = scaled_side(user_emb, user_cot, user_root)
    item_side = scaled_side(item_emb, item_cot, item_root)
    user_panel = lax.all_gather(user_side, "col", axis=0, tiled=True)
    item_panel = lax.all_gather(item_side, "row", axis=0, tiled=True)
    item_blocks = item_panel.shape[0] // block_size
    item_grid = item_panel.reshape(item_blocks, block_size, doubled)
    live_slots = jnp.arange(slot_count, dtype=jnp.int32)[None, :] < row_count
    live_cols = jnp.where(live_slots, tile_cols, item_blocks)
    user_blocks = user_panel.reshape(block_rows, block_size, doubled)
    tile_grid = tiles.reshape(block_rows, block_size, slot_count, block_size)
    user_partial, item_partial = padded_pass(tile_grid, live_cols, user_blocks, item_grid)
    user_total = lax.psum_scatter(user_partial, "col", scatter_dimension=0, tiled=True)
    item_total = lax.psum_scatter(item_partial, "row", scatter_dimension=0, tiled=True)
    user_out = user_total * user_root[:, None]
    item_out = item_total * item_root[:, None]
    return (user_out[:, :width], item_out[:, :width], user_out[:, width:], item_out[:, width:])


def solution(mesh):
    in_specs = (
        P(("row", "col"), None),
        P(("row", "col"), None),
        P(("row", "col"), None),
        P(("row", "col"), None),
        P("row", "col"),
        P("row", "col"),
        P("row", "col"),
        P(("row", "col")),
        P(("row", "col")),
    )
    out_specs = (
        P(("row", "col"), None),
        P(("row", "col"), None),
        P(("row", "col"), None),
        P(("row", "col"), None),
    )
    return jax.shard_map(shards, mesh=mesh, in_specs=in_specs, out_specs=out_specs, check_vma=False)
```

profile of v0, /device:TPU:0, one launch (start us, length us, event | category | flops | bytes accessed | tf_op | source)
XLA Modules:
  0.0 184.4 jit_solution(7699973863557302196)
XLA Ops:
  7.2 0.7 convert_rsqrt_fusion
  7.9 1.8 multiply_convert_fusion
  9.7 0.0 all-gather.3.cloned.1.call-start
  9.8 0.7 convert_rsqrt_fusion.1
  10.4 1.8 multiply_convert_fusion.1
  12.2 0.0 reduce-scatter.5.cloned.1.call-start
  12.3 0.7 fusion.22
  13.0 0.1 copy.24
  13.1 7.0 %reshape.33 = bf16[2,8,128,5,128]{4,3,2,1,0:T(8,128)(2,1)} reshape(bf16[2048,640]{1,0:T(8,128)(2,1)} %param.15) | data formatting | bytes 5242880 | tf_op jit(solution)/shard_map/reshape;reshape | solution.py:35
  20.1 19.7 %all-gather.5.cloned.1.call-done = bf16[1024,512]{1,0:T(8,128)(2,1)} async-done(((bf16[256,512]{1,0:T(8,128)(2,1)}), bf16[1024,512]{1,0:T(8,128)(2,1)}) %all-gather.5.cloned.1.call-update) | async-done | bytes 1048592 | tf_op jit(solution)/shard_map/all_gather | solution.py:61
  39.8 31.3 %all-gather.3.cloned.1.call-done = bf16[2048,512]{1,0:T(8,128)(2,1)} async-done(((bf16[256,512]{1,0:T(8,128)(2,1)}), bf16[2048,512]{1,0:T(8,128)(2,1)}) %all-gather.3.cloned.1.call-update) | async-done | bytes 2097168 | tf_op jit(solution)/shard_map/all_gather | solution.py:60
  71.1 16.3 %while.13 = (s32[]{:T(128)}, f32[8,128,512]{2,1,0:T(8,128)S(1)}, f32[2,8,128,512]{3,2,1,0:T(8,128)}, s32[2,8,5]{2,1,0:T(8,128)S(1)}, bf16[2,8,128,5,128]{4,3,2,1...) while((s32[]{:T(128)}, f32[8,128,512]{2,1,0:T(8,128)S(1)}, ...), condition=%wide.region_1.2_spmd.clone, body=%wide.region_0.1_spmd.clone.sunk | while | flops 2159018496 | bytes 62915276 | solution.py:46
  71.1 2.4 %fusion.38 = bf16[8,128,8,128]{3,2,1,0:T(8,128)(2,1)S(1)} fusion(bf16[2,8,128,5,128]{4,3,2,1,0:T(8,128)(2,1)} %get-tuple-element.165, s32[]{:T(128)S(6)} %copy.42, s32[8,5]{1,0:T(8,128)S(1)} %dynamic-slice_bitcast_fusion.2), kind=kOutput, calls=%fused_computation.9.clone.1 | convolution fusion | flops 10486080 | bytes 4194468 | tf_op jit(solution)/shard_map/while/body/eval_jaxpr/gikj,gkc->gicj/dot_general | solution.py:18
  73.5 1.5 bitcast_add_fusion.2
  75.0 0.7 copy-done.2
  75.7 0.3 copy-done.4
  76.0 1.2 bitcast_dynamic-update-slice_fusion.2
  77.3 2.0 %copy-done.3 = f32[2,8,128,512]{3,2,1,0:T(8,128)} copy-done((f32[2,8,128,512]{3,2,1,0:T(8,128)}, f32[2,8,128,512]{3,2,1,0:T(8,128)S(1)}, u32[]{:S(2)}) %copy-start.3) | copy-done | bytes 4194328 | tf_op jit(solution)/shard_map/while
  79.2 2.4 %fusion.38 = bf16[8,128,8,128]{3,2,1,0:T(8,128)(2,1)S(1)} fusion(bf16[2,8,128,5,128]{4,3,2,1,0:T(8,128)(2,1)} %get-tuple-element.165, s32[]{:T(128)S(6)} %copy.42, s32[8,5]{1,0:T(8,128)S(1)} %dynamic-slice_bitcast_fusion.2), kind=kOutput, calls=%fused_computation.9.clone.1 | convolution fusion | flops 10486080 | bytes 4194468 | tf_op jit(solution)/shard_map/while/body/eval_jaxpr/gikj,gkc->gicj/dot_general | solution.py:18
  81.7 1.5 bitcast_add_fusion.2
  83.2 0.7 copy-done.2
  83.9 0.3 copy-done.4
  84.2 1.2 bitcast_dynamic-update-slice_fusion.2
  85.4 2.0 %copy-done.3 = f32[2,8,128,512]{3,2,1,0:T(8,128)} copy-done((f32[2,8,128,512]{3,2,1,0:T(8,128)}, f32[2,8,128,512]{3,2,1,0:T(8,128)S(1)}, u32[]{:S(2)}) %copy-start.3) | copy-done | bytes 4194328 | tf_op jit(solution)/shard_map/while
  87.4 1.3 copy-done
  88.8 0.5 reduce-scatter.3.cloned.1.call-update
  89.3 34.2 %reduce-scatter.5.cloned.1.call-done = f32[256,512]{1,0:T(8,128)} async-done(((f32[1024,512]{1,0:T(8,128)}), f32[256,512]{1,0:T(8,128)}) %reduce-scatter.5.cloned.1.call-update) | async-done | bytes 524304 | tf_op jit(solution)/shard_map/reduce_scatter | solution.py:70
  123.6 1.1 broadcast_multiply_fusion
  124.7 0.8 fusion.23
  125.5 50.3 %reduce-scatter.3.cloned.1.call-done = f32[256,512]{1,0:T(8,128)} async-done(((f32[2048,512]{1,0:T(8,128)}), f32[256,512]{1,0:T(8,128)}) %reduce-scatter.3.cloned.1.call-update) | async-done | bytes 524304 | tf_op jit(solution)/shard_map/reduce_scatter | solution.py:69
  175.9 1.1 broadcast_multiply_fusion.1
  177.0 0.8 fusion.24
  (20 shorter events, 0.2 us)
Async XLA Ops:
  7.2 32.6 %all-gather.5.cloned.1.call-start = ((), (), s32[]{:S(2)}) async-start(), calls=%async_computation.3 | async-start | bytes 1310720 | tf_op jit(solution)/shard_map/all_gather | solution.py:61
  9.7 61.4 %all-gather.3.cloned.1.call-start = ((), (), s32[]{:S(2)}) async-start(), calls=%async_computation.2 | async-start | bytes 2359296 | tf_op jit(solution)/shard_map/all_gather | solution.py:60
  12.2 111.3 %reduce-scatter.5.cloned.1.call-start = ((), (), s32[]{:S(2)}) async-start(), calls=%async_computation.5 | async-start | bytes 2621440 | tf_op jit(solution)/shard_map/reduce_scatter | solution.py:70
  71.1 2.4 %copy-start.1 = (bf16[2,8,128,512]{3,2,1,0:T(8,128)(2,1)S(1)}, bf16[2,8,128,512]{3,2,1,0:T(8,128)(2,1)}, u32[]{:S(2)}) copy-start(bf16[2,8,128,512]{3,2,1,0:T(8,128)(2,1)} %get-tuple-element.166) | copy-start | bytes 6291460 | tf_op jit(solution)/shard_map/while
  73.5 2.2 %copy-start.2 = (f32[2,8,128,512]{3,2,1,0:T(8,128)S(1)}, f32[2,8,128,512]{3,2,1,0:T(8,128)}, u32[]{:S(2)}) copy-start(f32[2,8,128,512]{3,2,1,0:T(8,128)} %get-tuple-element.154) | copy-start | bytes 12582916 | tf_op jit(solution)/shard_map/while
  73.5 2.5 %copy-start.4 = (bf16[8,128,512]{2,1,0:T(8,128)(2,1)S(1)}, bf16[8,128,512]{2,1,0:T(8,128)(2,1)}, u32[]{:S(2)}) copy-start(bf16[8,128,512]{2,1,0:T(8,128)(2,1)} %get-tuple-element.167) | copy-start | bytes 3145732 | tf_op jit(solution)/shard_map/while
  77.3 2.0 %copy-start.3 = (f32[2,8,128,512]{3,2,1,0:T(8,128)}, f32[2,8,128,512]{3,2,1,0:T(8,128)S(1)}, u32[]{:S(2)}) copy-start(f32[2,8,128,512]{3,2,1,0:T(8,128)S(1)} %bitcast_dynamic-update-slice_fusion.2) | copy-start | bytes 12582916 | tf_op jit(solution)/shard_map/while
  79.2 2.4 %copy-start.1 = (bf16[2,8,128,512]{3,2,1,0:T(8,128)(2,1)S(1)}, bf16[2,8,128,512]{3,2,1,0:T(8,128)(2,1)}, u32[]{:S(2)}) copy-start(bf16[2,8,128,512]{3,2,1,0:T(8,128)(2,1)} %get-tuple-element.166) | copy-start | bytes 6291460 | tf_op jit(solution)/shard_map/while
  81.7 2.2 %copy-start.2 = (f32[2,8,128,512]{3,2,1,0:T(8,128)S(1)}, f32[2,8,128,512]{3,2,1,0:T(8,128)}, u32[]{:S(2)}) copy-start(f32[2,8,128,512]{3,2,1,0:T(8,128)} %get-tuple-element.154) | copy-start | bytes 12582916 | tf_op jit(solution)/shard_map/while
  81.7 2.5 %copy-start.4 = (bf16[8,128,512]{2,1,0:T(8,128)(2,1)S(1)}, bf16[8,128,512]{2,1,0:T(8,128)(2,1)}, u32[]{:S(2)}) copy-start(bf16[8,128,512]{2,1,0:T(8,128)(2,1)} %get-tuple-element.167) | copy-start | bytes 3145732 | tf_op jit(solution)/shard_map/while
  85.4 2.0 %copy-start.3 = (f32[2,8,128,512]{3,2,1,0:T(8,128)}, f32[2,8,128,512]{3,2,1,0:T(8,128)S(1)}, u32[]{:S(2)}) copy-start(f32[2,8,128,512]{3,2,1,0:T(8,128)S(1)} %bitcast_dynamic-update-slice_fusion.2) | copy-start | bytes 12582916 | tf_op jit(solution)/shard_map/while
  87.4 1.3 copy-start
  88.7 87.1 %reduce-scatter.3.cloned.1.call-start = ((), (), s32[]{:S(2)}) async-start(), calls=%async_computation.4 | async-start | bytes 4718592 | tf_op jit(solution)/shard_map/reduce_scatter | solution.py:69
Sparse Core Ops, SparseCore 0:
  10.4 29.3 all-gather.4
  41.9 29.0 all-gather.2
  88.9 34.6 reduce-scatter.4
  125.8 49.9 reduce-scatter.2
where the time goes:
time: 185 us; the launch traced here: 184 us
  waiting for transfers between devices  136 us (74%)
  local copies, waits for them, and re-layouts  16 us (9%)
  between operations  13.8 us (7%)
  matrix products  10.3 us (6%)
  other arithmetic  7.91 us (4%)
    reduce_scatter x1, waiting for transfers between devices, shards(): lax.psum_scatter(user_partial, 'col', scatter_dimension=0, tiled=True)  50.3 us
    reduce_scatter x1, waiting for transfers between devices, shards(): lax.psum_scatter(item_partial, 'row', scatter_dimension=0, tiled=True)  34.2 us
    all_gather x1, waiting for transfers between devices, shards(): user_panel = lax.all_gather(user_side, 'col', axis=0, tiled=True)  31.3 us
    all_gather x1, waiting for transfers between devices, shards(): item_panel = lax.all_gather(item_side, 'row', axis=0, tiled=True)  19.7 us
    another operation x1, local copies, waits for them, and re-layouts, padded_pass(): tile_grid.reshape(turn_count, group_size, block_size, slot_count, block_s...  6.98 us
    while x16, local copies, waits for them, and re-layouts  5.95 us
    dot_general x2, matrix products, spread_rows(): return jnp.einsum('gikj,gkc->gicj', tile_group, selector)  4.86 us
  transfers between devices with their start and end apart: 4, of which 4 were waited for; matrix products, arithmetic and copies ran while one was open for 7% of the time, Pallas kernels for 0%

commit v1 on v0

v1 whole, which is shorter than its diff:
```python
import functools

import jax
import jax.numpy as jnp
from jax import lax
from jax.experimental import pallas as pl
from jax.experimental.pallas import tpu as pltpu
from jax.sharding import PartitionSpec as P

VMEM_BYTES = 40 * 1024 * 1024


def swap(value, axis, count, mask):
    return lax.ppermute(value, axis, [(i, i ^ mask) for i in range(count)])


def full(shape):
    return pl.BlockSpec(shape, lambda *_: (0,) * len(shape))


def params():
    return pltpu.CompilerParams(vmem_limit_bytes=VMEM_BYTES)


def cost(rows, depth, columns):
    return pl.CostEstimate(
        flops=2 * rows * depth * columns,
        bytes_accessed=2 * (rows * depth + depth * columns + rows * columns),
        transcendentals=0,
    )


def dense_kernel(block, slots, order, cols, counts, place, tiles_ref, dense_ref, turned_ref):
    dense_ref[...] = jnp.zeros_like(dense_ref)
    turned_ref[...] = jnp.zeros_like(turned_ref)
    row = order[pl.program_id(0)]
    for k in range(slots):

        @pl.when(k < counts[row, 0])
        def _():
            at = pl.multiple_of(place[cols[row, k]] * block, block)
            tile = tiles_ref[:, k * block : (k + 1) * block]
            dense_ref[:, pl.ds(at, block)] = tile
            turned_ref[pl.ds(at, block), :] = tile.T


def densify(tiles, tile_cols, row_count, order, place, item_blocks):
    block_rows, slots = tile_cols.shape
    block = tiles.shape[0] // block_rows
    items = item_blocks * block
    grid_spec = pltpu.PrefetchScalarGridSpec(
        num_scalar_prefetch=4,
        grid=(block_rows,),
        in_specs=[pl.BlockSpec((block, slots * block), lambda b, order, *_: (order[b], 0))],
        out_specs=[
            pl.BlockSpec((block, items), lambda b, *_: (b, 0)),
            pl.BlockSpec((items, block), lambda b, *_: (0, b)),
        ],
    )
    return pl.pallas_call(
        functools.partial(dense_kernel, block, slots),
        grid_spec=grid_spec,
        out_shape=[
            jax.ShapeDtypeStruct((block_rows * block, items), tiles.dtype),
            jax.ShapeDtypeStruct((items, block_rows * block), tiles.dtype),
        ],
        compiler_params=params(),
        name="densify",
    )(order, tile_cols, row_count, place, tiles)


def gather_scratch(parts, whole):
    rows = parts[0].shape[0]
    for i, part in enumerate(parts):
        whole[i * rows : (i + 1) * rows, :] = part[...]


def products(matrix, row_of, parts, added=None):
    rows, width = parts[0].shape
    depth = len(parts) * rows
    steps = len(row_of)
    stride = row_of[1] - row_of[0] if steps > 1 else 1
    base = row_of[0]
    count = len(parts)

    def kernel(*refs):
        matrix_ref, part_refs = refs[0], refs[1 : 1 + count]
        rest = refs[1 + count :]
        if added is not None:
            added_ref, rest = rest[0], rest[1:]
        outs, whole = rest[:steps], rest[steps]
        step = pl.program_id(0)

        @pl.when(step == 0)
        def _():
            gather_scratch(part_refs, whole)

        total = jnp.dot(matrix_ref[...], whole[...], preferred_element_type=jnp.float32)
        if added is not None:
            total = total + added_ref[...].astype(jnp.float32)
        for s, out in enumerate(outs):

            @pl.when(step == s)
            def _(out=out):
                out[...] = total.astype(out.dtype)

    in_specs = [pl.BlockSpec((rows, depth), lambda s: (base + stride * s, 0))]
    in_specs += [full((rows, width))] * count
    operands = [matrix, *parts]
    if added is not None:
        in_specs.append(pl.BlockSpec((rows, width), lambda s: (s, 0)))
        operands.append(added)
    kinds = [jnp.float32 if s == 0 else jnp.bfloat16 for s in range(steps)]
    return pl.pallas_call(
        kernel,
        grid=(steps,),
        in_specs=in_specs,
        out_specs=[full((rows, width))] * steps,
        out_shape=[jax.ShapeDtypeStruct((rows, width), kind) for kind in kinds],
        scratch_shapes=[pltpu.VMEM((depth, width), jnp.bfloat16)],
        compiler_params=params(),
        cost_estimate=cost(steps * rows, depth, width),
        name="products",
    )(*operands)


def stacked_products(matrix, row_of, parts):
    rows, width = parts[0].shape
    depth = len(parts) * rows
    steps = len(row_of)
    stride = row_of[1] - row_of[0] if steps > 1 else 1
    base = row_of[0]
    count = len(parts)

    def kernel(*refs):
        matrix_ref, part_refs, out, whole = refs[0], refs[1 : 1 + count], refs[1 + count], refs[2 + count]

        @pl.when(pl.program_id(0) == 0)
        def _():
            gather_scratch(part_refs, whole)

        out[...] = jnp.dot(matrix_ref[...], whole[...], preferred_element_type=jnp.float32).astype(out.dtype)

    return pl.pallas_call(
        kernel,
        grid=(steps,),
        in_specs=[pl.BlockSpec((rows, depth), lambda s: (base + stride * s, 0))] + [full((rows, width))] * count,
        out_specs=pl.BlockSpec((rows, width), lambda s: (s, 0)),
        out_shape=jax.ShapeDtypeStruct((steps * rows, width), jnp.bfloat16),
        scratch_shapes=[pltpu.VMEM((depth, width), jnp.bfloat16)],
        compiler_params=params(),
        cost_estimate=cost(steps * rows, depth, width),
        name="stacked_products",
    )(matrix, *parts)


def finish(own, others, root):
    rows, width = own.shape

    def kernel(*refs):
        own_ref, root_ref, other_refs, (left, right) = refs[0], refs[1], refs[2:-2], refs[-2:]
        total = own_ref[...]
        for other in other_refs:
            total = total + other[...].astype(jnp.float32)
        total = total * root_ref[...]
        left[...] = total[:, : width // 2]
        right[...] = total[:, width // 2 :]

    return pl.pallas_call(
        kernel,
        out_shape=[jax.ShapeDtypeStruct((rows, width // 2), jnp.float32)] * 2,
        compiler_params=params(),
        cost_estimate=pl.CostEstimate(
            flops=rows * width * (len(others) + 1), bytes_accessed=rows * width * (8 + 2 * len(others)), transcendentals=0
        ),
        name="finish",
    )(own, root, *others)


def scaled_side(former, latter, root):
    joined = jnp.concatenate([former, latter], axis=1).astype(jnp.float32)
    return (joined * root).astype(jnp.bfloat16)


def shards(n_row, n_col, user_emb, item_emb, user_cot, item_cot, tiles, tile_cols, row_count, user_deg, item_deg):
    block_rows, slots = tile_cols.shape
    block = tiles.shape[0] // block_rows
    here_row, here_col = lax.axis_index("row"), lax.axis_index("col")
    item_rows = item_emb.shape[0]
    user_rows = user_emb.shape[0]
    item_blocks = n_row * item_rows // block
    per_item, per_user = item_rows // block, user_rows // block

    user_root = 1.0 / jnp.sqrt(user_deg.astype(jnp.float32))[:, None]
    item_root = 1.0 / jnp.sqrt(item_deg.astype(jnp.float32))[:, None]
    item_side = scaled_side(item_emb, item_cot, item_root)
    user_side = scaled_side(user_emb, user_cot, user_root)

    item_parts = [item_side] + [swap(item_side, "row", n_row, k) for k in range(1, n_row)]
    user_even = [user_side] + [swap(user_side, "col", n_col, 2 * j) for j in range(1, n_col // 2)]
    user_parts = []
    for part in user_even:
        user_parts += [part, swap(part, "col", n_col, 1)]

    block_ids = jnp.arange(block_rows, dtype=jnp.int32)
    order = ((block_ids // per_user) ^ here_col) * per_user + block_ids % per_user
    item_ids = jnp.arange(item_blocks, dtype=jnp.int32)
    place = ((item_ids // per_item) ^ here_row) * per_item + item_ids % per_item
    dense, turned = densify(tiles, tile_cols, row_count, order, place, item_blocks)

    to_sibling = stacked_products(dense, list(range(1, n_col, 2)), item_parts)
    from_sibling = swap(to_sibling, "col", n_col, 1)
    user_sums = products(dense, list(range(0, n_col, 2)), item_parts, from_sibling)
    user_others = [swap(user_sums[j], "col", n_col, 2 * j) for j in range(1, n_col // 2)]

    item_sums = products(turned, list(range(n_row)), user_parts)
    item_others = [swap(item_sums[k], "row", n_row, k) for k in range(1, n_row)]

    user_next, user_grad = finish(user_sums[0], user_others, user_root)
    item_next, item_grad = finish(item_sums[0], item_others, item_root)
    return (user_next, item_next, user_grad, item_grad)


def solution(mesh):
    nodes = P(("row", "col"), None)
    in_specs = (nodes,) * 4 + (P("row", "col"),) * 3 + (P(("row", "col")),) * 2
    body = functools.partial(shards, mesh.shape["row"], mesh.shape["col"])
    return jax.shard_map(body, mesh=mesh, in_specs=in_specs, out_specs=(nodes,) * 4, check_vma=False)
```

time: 185 us -> 84.4 us (0.46)
  the two profiles are of different devices: /device:TPU:0 before, /device:TPU:16 now
where the time goes in v1:
time: 84.4 us; the launch traced here: 84.2 us
  waiting for transfers between devices  49.7 us (59%)
  starting transfers between devices  13.9 us (16%)
  Pallas kernels  13.8 us (16%)
  local copies, waits for them, and re-layouts  3.51 us (4%)
  other arithmetic  2.56 us (3%)
    ppermute x17, waiting for transfers between devices, swap(): return lax.ppermute(value, axis, [(i, i ^ mask) for i in range(count)])  49.7 us
    ppermute x17, starting transfers between devices, swap(): return lax.ppermute(value, axis, [(i, i ^ mask) for i in range(count)])  13.9 us
    pallas_call x2, Pallas kernels, products(): pl.pallas_call(kernel, grid=(steps,), in_specs=in_specs, out_specs=[full(...  5.99 us
    pallas_call x1, Pallas kernels, densify(): pl.pallas_call(functools.partial(dense_kernel, block, slots), grid_spec=g...  4.12 us
    unnamed x8, local copies, waits for them, and re-layouts  3.24 us
    pallas_call x1, Pallas kernels, stacked_products(): pl.pallas_call(kernel, grid=(steps,), in_specs=[pl.BlockSpec((rows, depth...  1.85 us
    pallas_call x2, Pallas kernels, finish(): pl.pallas_call(kernel, out_shape=[jax.ShapeDtypeStruct((rows, width // 2)...  1.83 us
  transfers between devices with their start and end apart: 17, of which 10 were waited for; matrix products, arithmetic and copies ran while one was open for 3% of the time, Pallas kernels for 13%

profile of v1, /device:TPU:16, one launch (start us, length us, event | category | flops | bytes accessed | tf_op | source)
XLA Modules:
  0.0 84.2 jit_solution(5804178112003769307)
XLA Ops:
  0.6 0.7 convert_rsqrt_fusion.1
  1.3 1.1 %multiply_convert_fusion.1.refs_1_ = bf16[256,512]{1,0:T(8,128)(2,1)S(1)} fusion(bf16[256,256]{1,0:T(8,128)(2,1)} %param.12, bf16[256,256]{1,0:T(8,128)(2,1)} %param.10, f32[256]{0:T(256)S(1)} %convert_rsqrt_fusion.1), kind=kLoop, calls=%fused_computation.1 | loop fusion | flops 786432 | bytes 525312 | tf_op jit(solution)/shard_map/convert_element_type | solution.py:182
  2.4 1.6 %collective-permute-start = (bf16[256,512]{1,0:T(8,128)(2,1)S(1)}, bf16[256,512]{1,0:T(8,128)(2,1)S(1)}, u32[]{:S(2)}, u32[]{:S(2)}) collective-permute-start(bf16[256,512]{1,0:T(8,128)(2,1)S(1)} %multiply_convert_fusion.1.refs_1_), channel_id=1, source_target_pairs={{0,8},{8,0},{16,24},{24,16},{1,9},{9,1},{17,25},{25,17},{2,10},{10... | collective-permute-start | bytes 786440 | tf_op jit(solution)/shard_map/ppermute | solution.py:14
  4.0 1.5 %collective-permute-start.1 = (bf16[256,512]{1,0:T(8,128)(2,1)S(1)}, bf16[256,512]{1,0:T(8,128)(2,1)S(1)}, u32[]{:S(2)}, u32[]{:S(2)}) collective-permute-start(bf16[256,512]{1,0:T(8,128)(2,1)S(1)} %multiply_convert_fusion.1.refs_1_), channel_id=1, source_target_pairs={{0,16},{8,24},{16,0},{24,8},{1,17},{9,25},{17,1},{25,9},{2,18},{10... | collective-permute-start | bytes 786440 | tf_op jit(solution)/shard_map/ppermute | solution.py:14
  5.5 0.5 collective-permute-start.2
  6.0 0.8 copy.15.cols
  6.7 0.7 copy.16.counts
  7.5 1.7 %copy-done = bf16[2048,640]{1,0:T(8,128)(2,1)S(1)} copy-done((bf16[2048,640]{1,0:T(8,128)(2,1)S(1)}, bf16[2048,640]{1,0:T(8,128)(2,1)}, u32[]{:S(2)}) %copy-start) | copy-done | bytes 2621464
  9.2 4.1 %densify.1 = (bf16[2048,1024]{1,0:T(8,128)(2,1)S(1)}, bf16[1024,2048]{1,0:T(8,128)(2,1)S(1)}) custom-call(s32[16]{0:T(128)S(1)} %fusion.order, s32[16,5]{1,0:T(8,128)S(1)} %copy.15.cols, s32[16,1]{1,0:T(8,128)S(1)} %copy.16.counts, s32[8]{0:T(128)S(1)} %fusion.1.place, bf16[2048,640]{1,0:T(8,128)(2,1)S(1)} %copy-done), custom_call_target="tpu_custom_call" | custom-call | tf_op jit(solution)/shard_map/densify/pallas_call | solution.py:60
  13.3 0.7 convert_rsqrt_fusion
  14.0 3.3 %collective-permute-done.1.refs_3_ = bf16[256,512]{1,0:T(8,128)(2,1)S(1)} collective-permute-done((bf16[256,512]{1,0:T(8,128)(2,1)S(1)}, bf16[256,512]{1,0:T(8,128)(2,1)S(1)}, u32[]{:S(2)}, u32[]{:S(2)}) %collective-permute-start.1) | collective-permute-done | bytes 262176 | tf_op jit(solution)/shard_map/ppermute | solution.py:14
  17.3 1.9 %stacked_products.1 = bf16[1024,512]{1,0:T(8,128)(2,1)S(1)} custom-call(bf16[2048,1024]{1,0:T(8,128)(2,1)S(1)} %get-tuple-element.18.refs_0_, bf16[256,512]{1,0:T(8,128)(2,1)S(1)} %multiply_convert_fusion.1.refs_1_, bf16[256,512]{1,0:T(8,128)(2,1)S(1)} %collective-permute-done.refs_2_, bf16[256,512]{1,0:T(8,128)(2,1)S(1)} %collective-permute-done.1.refs_3_, ...), custom_call_target="tpu_custom_call" | custom-call | flops 1073741824 | bytes 4194304 | tf_op jit(solution)/shard_map/stacked_products/pallas_call | solution.py:144
  19.8 2.7 %collective-permute-start.12 = (bf16[256,512]{1,0:T(8,128)(2,1)S(1)}, bf16[256,512]{1,0:T(8,128)(2,1)S(1)}, u32[]{:S(2)}, u32[]{:S(2)}) collective-permute-start(bf16[256,512]{1,0:T(8,128)(2,1)S(1)} %multiply_convert_fusion.refs_1_), channel_id=1, source_target_pairs={{0,6},{1,7},{2,4},{3,5},{4,2},{5,3},{6,0},{7,1},{8,14},{9,15},{10,... | collective-permute-start | bytes 786440 | tf_op jit(solution)/shard_map/ppermute | solution.py:14
  22.5 1.3 %collective-permute-start.8 = (bf16[256,512]{1,0:T(8,128)(2,1)S(1)}, bf16[256,512]{1,0:T(8,128)(2,1)S(1)}, u32[]{:S(2)}, u32[]{:S(2)}) collective-permute-start(bf16[256,512]{1,0:T(8,128)(2,1)S(1)} %multiply_convert_fusion.refs_1_), channel_id=1, source_target_pairs={{0,2},{1,3},{2,0},{3,1},{4,6},{5,7},{6,4},{7,5},{8,10},{9,11},{10,... | collective-permute-start | bytes 786440 | tf_op jit(solution)/shard_map/ppermute | solution.py:14
  23.9 13.8 %collective-permute-done.10.refs_5_ = bf16[256,512]{1,0:T(8,128)(2,1)S(1)} collective-permute-done((bf16[256,512]{1,0:T(8,128)(2,1)S(1)}, bf16[256,512]{1,0:T(8,128)(2,1)S(1)}, u32[]{:S(2)}, u32[]{:S(2)}) %collective-permute-start.10) | collective-permute-done | bytes 262176 | tf_op jit(solution)/shard_map/ppermute | solution.py:14
  37.7 8.2 %collective-permute-done.12.refs_7_ = bf16[256,512]{1,0:T(8,128)(2,1)S(1)} collective-permute-done((bf16[256,512]{1,0:T(8,128)(2,1)S(1)}, bf16[256,512]{1,0:T(8,128)(2,1)S(1)}, u32[]{:S(2)}, u32[]{:S(2)}) %collective-permute-start.12) | collective-permute-done | bytes 262176 | tf_op jit(solution)/shard_map/ppermute | solution.py:14
  46.0 0.4 collective-permute-start.9
  46.5 1.0 %collective-permute-done.13.refs_8_ = bf16[256,512]{1,0:T(8,128)(2,1)S(1)} collective-permute-done((bf16[256,512]{1,0:T(8,128)(2,1)S(1)}, bf16[256,512]{1,0:T(8,128)(2,1)S(1)}, u32[]{:S(2)}, u32[]{:S(2)}) %collective-permute-start.13) | collective-permute-done | bytes 262176 | tf_op jit(solution)/shard_map/ppermute | solution.py:14
  47.9 3.1 %products.3 = (f32[256,512]{1,0:T(8,128)S(1)}, bf16[256,512]{1,0:T(8,128)(2,1)S(1)}, bf16[256,512]{1,0:T(8,128)(2,1)S(1)}, bf16[256,512]{1,0:T(8,128)(2,1)S(1)}) custom-call(bf16[1024,2048]{1,0:T(8,128)(2,1)S(1)} %get-tuple-element.24.refs_0_, bf16[256,512]{1,0:T(8,128)(2,1)S(1)} %multiply_convert_fusion.refs_1_, ...), custom_call_target="tpu_custom_call" | custom-call | flops 2147483648 | bytes 7340032 | tf_op jit(solution)/shard_map/products/pallas_call | solution.py:114
  51.0 1.3 %collective-permute-start.14 = (bf16[256,512]{1,0:T(8,128)(2,1)S(1)}, bf16[256,512]{1,0:T(8,128)(2,1)S(1)}, u32[]{:S(2)}, u32[]{:S(2)}) collective-permute-start(bf16[256,512]{1,0:T(8,128)(2,1)S(1)} %get-tuple-element.26), channel_id=1, source_target_pairs={{0,8},{8,0},{16,24},{24,16},{1,9},{9,1},{17,25},{25,17},{2,10},{10... | collective-permute-start | bytes 786440 | tf_op jit(solution)/shard_map/ppermute | solution.py:14
  52.3 0.8 collective-permute-start.15
  53.1 1.4 %collective-permute-start.16 = (bf16[256,512]{1,0:T(8,128)(2,1)S(1)}, bf16[256,512]{1,0:T(8,128)(2,1)S(1)}, u32[]{:S(2)}, u32[]{:S(2)}) collective-permute-start(bf16[256,512]{1,0:T(8,128)(2,1)S(1)} %get-tuple-element.28), channel_id=1, source_target_pairs={{0,24},{8,16},{16,8},{24,0},{1,25},{9,17},{17,9},{25,1},{2,26},{10... | collective-permute-start | bytes 786440 | tf_op jit(solution)/shard_map/ppermute | solution.py:14
  54.6 2.9 %products.2 = (f32[256,512]{1,0:T(8,128)S(1)}, bf16[256,512]{1,0:T(8,128)(2,1)}, bf16[256,512]{1,0:T(8,128)(2,1)}, bf16[256,512]{1,0:T(8,128)(2,1)}) custom-call(bf16[2048,1024]{1,0:T(8,128)(2,1)S(1)} %get-tuple-element.18.refs_0_, bf16[256,512]{1,0:T(8,128)(2,1)S(1)} %multiply_convert_fusion.1.refs_1_, bf16[256,512]{1,0:T(8,128)(2,1)S(1)} %collective-permute-done.refs_2_, ...), custom_call_target="tpu_custom_call" | custom-call | flops 1073741824 | bytes 4194304 | tf_op jit(solution)/shard_map/products/pallas_call | solution.py:114
  57.4 1.0 %collective-permute-start.5 = (bf16[256,512]{1,0:T(8,128)(2,1)}, bf16[256,512]{1,0:T(8,128)(2,1)S(1)}, u32[]{:S(2)}, u32[]{:S(2)}) collective-permute-start(bf16[256,512]{1,0:T(8,128)(2,1)} %get-tuple-element.21), channel_id=1, source_target_pairs={{0,4},{1,5},{2,6},{3,7},{4,0},{5,1},{6,2},{7,3},{8,12},{9,13},{10,... | collective-permute-start | bytes 786440 | tf_op jit(solution)/shard_map/ppermute | solution.py:14
  58.5 1.7 %collective-permute-done.14.refs_2_ = bf16[256,512]{1,0:T(8,128)(2,1)S(1)} collective-permute-done((bf16[256,512]{1,0:T(8,128)(2,1)S(1)}, bf16[256,512]{1,0:T(8,128)(2,1)S(1)}, u32[]{:S(2)}, u32[]{:S(2)}) %collective-permute-start.14) | collective-permute-done | bytes 262176 | tf_op jit(solution)/shard_map/ppermute | solution.py:14
  60.2 0.7 collective-permute-start.6
  61.2 3.1 %collective-permute-done.15.refs_3_ = bf16[256,512]{1,0:T(8,128)(2,1)S(1)} collective-permute-done((bf16[256,512]{1,0:T(8,128)(2,1)S(1)}, bf16[256,512]{1,0:T(8,128)(2,1)S(1)}, u32[]{:S(2)}, u32[]{:S(2)}) %collective-permute-start.15) | collective-permute-done | bytes 262176 | tf_op jit(solution)/shard_map/ppermute | solution.py:14
  64.4 1.6 %collective-permute-done.16.refs_4_ = bf16[256,512]{1,0:T(8,128)(2,1)S(1)} collective-permute-done((bf16[256,512]{1,0:T(8,128)(2,1)S(1)}, bf16[256,512]{1,0:T(8,128)(2,1)S(1)}, u32[]{:S(2)}, u32[]{:S(2)}) %collective-permute-start.16) | collective-permute-done | bytes 262176 | tf_op jit(solution)/shard_map/ppermute | solution.py:14
  66.0 0.9 %finish.3 = (f32[256,256]{1,0:T(8,128)}, f32[256,256]{1,0:T(8,128)}) custom-call(f32[256,512]{1,0:T(8,128)S(1)} %get-tuple-element.25.refs_0_, f32[256,1]{1,0:T(8,128)S(1)} %copy.18.refs_1_, bf16[256,512]{1,0:T(8,128)(2,1)S(1)} %collective-permute-done.14.refs_2_, bf16[256,512]{1,0:T(8,128)(2,1)S(1)} %collective-permute-done.15.refs_3_, ...), custom_call_target="tpu_custom_call" | custom-call | flops 524288 | bytes 1835008 | tf_op jit(solution)/shard_map/finish/pallas_call | solution.py:169
  66.9 9.9 %collective-permute-done.5.refs_3_ = bf16[256,512]{1,0:T(8,128)(2,1)S(1)} collective-permute-done((bf16[256,512]{1,0:T(8,128)(2,1)}, bf16[256,512]{1,0:T(8,128)(2,1)S(1)}, u32[]{:S(2)}, u32[]{:S(2)}) %collective-permute-start.5) | collective-permute-done | bytes 262176 | tf_op jit(solution)/shard_map/ppermute | solution.py:14
  76.8 6.5 %collective-permute-done.6.refs_4_ = bf16[256,512]{1,0:T(8,128)(2,1)S(1)} collective-permute-done((bf16[256,512]{1,0:T(8,128)(2,1)}, bf16[256,512]{1,0:T(8,128)(2,1)S(1)}, u32[]{:S(2)}, u32[]{:S(2)}) %collective-permute-start.6) | collective-permute-done | bytes 262176 | tf_op jit(solution)/shard_map/ppermute | solution.py:14
  83.2 0.9 %finish.2 = (f32[256,256]{1,0:T(8,128)}, f32[256,256]{1,0:T(8,128)}) custom-call(f32[256,512]{1,0:T(8,128)S(1)} %get-tuple-element.19.refs_0_, f32[256,1]{1,0:T(8,128)S(1)} %copy.17.refs_1_, bf16[256,512]{1,0:T(8,128)(2,1)S(1)} %collective-permute-done.4.refs_2_, bf16[256,512]{1,0:T(8,128)(2,1)S(1)} %collective-permute-done.5.refs_3_, ...), custom_call_target="tpu_custom_call" | custom-call | flops 524288 | bytes 1835008 | tf_op jit(solution)/shard_map/finish/pallas_call | solution.py:169
  (24 shorter events, 1.3 us)
Async XLA Ops:
  2.4 11.6 %collective-permute-start = (bf16[256,512]{1,0:T(8,128)(2,1)S(1)}, bf16[256,512]{1,0:T(8,128)(2,1)S(1)}, u32[]{:S(2)}, u32[]{:S(2)}) collective-permute-start(bf16[256,512]{1,0:T(8,128)(2,1)S(1)} %multiply_convert_fusion.1.refs_1_), channel_id=1, source_target_pairs={{0,8},{8,0},{16,24},{24,16},{1,9},{9,1},{17,25},{25,17},{2,10},{10... | collective-permute-start | bytes 786440 | tf_op jit(solution)/shard_map/ppermute | solution.py:14
  4.0 13.4 %collective-permute-start.1 = (bf16[256,512]{1,0:T(8,128)(2,1)S(1)}, bf16[256,512]{1,0:T(8,128)(2,1)S(1)}, u32[]{:S(2)}, u32[]{:S(2)}) collective-permute-start(bf16[256,512]{1,0:T(8,128)(2,1)S(1)} %multiply_convert_fusion.1.refs_1_), channel_id=1, source_target_pairs={{0,16},{8,24},{16,0},{24,8},{1,17},{9,25},{17,1},{25,9},{2,18},{10... | collective-permute-start | bytes 786440 | tf_op jit(solution)/shard_map/ppermute | solution.py:14
  5.5 11.9 %collective-permute-start.2 = (bf16[256,512]{1,0:T(8,128)(2,1)S(1)}, bf16[256,512]{1,0:T(8,128)(2,1)S(1)}, u32[]{:S(2)}, u32[]{:S(2)}) collective-permute-start(bf16[256,512]{1,0:T(8,128)(2,1)S(1)} %multiply_convert_fusion.1.refs_1_), channel_id=1, source_target_pairs={{0,24},{8,16},{16,8},{24,0},{1,25},{9,17},{17,9},{25,1},{2,26},{10... | collective-permute-start | bytes 786440 | tf_op jit(solution)/shard_map/ppermute | solution.py:14
  7.5 1.7 %copy-start = (bf16[2048,640]{1,0:T(8,128)(2,1)S(1)}, bf16[2048,640]{1,0:T(8,128)(2,1)}, u32[]{:S(2)}) copy-start(bf16[2048,640]{1,0:T(8,128)(2,1)} %tiles_ref.1) | copy-start | bytes 7864324
  9.2 10.1 %copy-start.1 = (bf16[256,256]{1,0:T(8,128)(2,1)S(1)}, bf16[256,256]{1,0:T(8,128)(2,1)}, u32[]{:S(2)}) copy-start(bf16[256,256]{1,0:T(8,128)(2,1)} %param.11) | copy-start | bytes 393220
  9.2 10.1 %copy-start.2 = (bf16[256,256]{1,0:T(8,128)(2,1)S(1)}, bf16[256,256]{1,0:T(8,128)(2,1)}, u32[]{:S(2)}) copy-start(bf16[256,256]{1,0:T(8,128)(2,1)} %param.9) | copy-start | bytes 393220
  19.2 35.4 %collective-permute-start.3 = (bf16[1024,512]{1,0:T(8,128)(2,1)S(1)}, bf16[1024,512]{1,0:T(8,128)(2,1)S(1)}, u32[]{:S(2)}, u32[]{:S(2)}) collective-permute-start(bf16[1024,512]{1,0:T(8,128)(2,1)S(1)} %stacked_products.1), channel_id=1, source_target_pairs={{0,1},{1,0},{2,3},{3,2},{4,5},{5,4},{6,7},{7,6},{8,9},{9,8},{10,11... | collective-permute-start | bytes 3145736 | tf_op jit(solution)/shard_map/ppermute | solution.py:14
  19.4 18.3 %collective-permute-start.10 = (bf16[256,512]{1,0:T(8,128)(2,1)S(1)}, bf16[256,512]{1,0:T(8,128)(2,1)S(1)}, u32[]{:S(2)}, u32[]{:S(2)}) collective-permute-start(bf16[256,512]{1,0:T(8,128)(2,1)S(1)} %multiply_convert_fusion.refs_1_), channel_id=1, source_target_pairs={{0,4},{1,5},{2,6},{3,7},{4,0},{5,1},{6,2},{7,3},{8,12},{9,13},{10,... | collective-permute-start | bytes 786440 | tf_op jit(solution)/shard_map/ppermute | solution.py:14
  19.8 26.2 %collective-permute-start.12 = (bf16[256,512]{1,0:T(8,128)(2,1)S(1)}, bf16[256,512]{1,0:T(8,128)(2,1)S(1)}, u32[]{:S(2)}, u32[]{:S(2)}) collective-permute-start(bf16[256,512]{1,0:T(8,128)(2,1)S(1)} %multiply_convert_fusion.refs_1_), channel_id=1, source_target_pairs={{0,6},{1,7},{2,4},{3,5},{4,2},{5,3},{6,0},{7,1},{8,14},{9,15},{10,... | collective-permute-start | bytes 786440 | tf_op jit(solution)/shard_map/ppermute | solution.py:14
  22.5 23.5 %collective-permute-start.8 = (bf16[256,512]{1,0:T(8,128)(2,1)S(1)}, bf16[256,512]{1,0:T(8,128)(2,1)S(1)}, u32[]{:S(2)}, u32[]{:S(2)}) collective-permute-start(bf16[256,512]{1,0:T(8,128)(2,1)S(1)} %multiply_convert_fusion.refs_1_), channel_id=1, source_target_pairs={{0,2},{1,3},{2,0},{3,1},{4,6},{5,7},{6,4},{7,5},{8,10},{9,11},{10,... | collective-permute-start | bytes 786440 | tf_op jit(solution)/shard_map/ppermute | solution.py:14
  23.9 22.6 %collective-permute-start.7 = (bf16[256,512]{1,0:T(8,128)(2,1)S(1)}, bf16[256,512]{1,0:T(8,128)(2,1)S(1)}, u32[]{:S(2)}, u32[]{:S(2)}) collective-permute-start(bf16[256,512]{1,0:T(8,128)(2,1)S(1)} %multiply_convert_fusion.refs_1_), channel_id=1, source_target_pairs={{0,1},{1,0},{2,3},{3,2},{4,5},{5,4},{6,7},{7,6},{8,9},{9,8},{10,11... | collective-permute-start | bytes 786440 | tf_op jit(solution)/shard_map/ppermute | solution.py:14
  37.7 8.8 %collective-permute-start.11 = (bf16[256,512]{1,0:T(8,128)(2,1)S(1)}, bf16[256,512]{1,0:T(8,128)(2,1)S(1)}, u32[]{:S(2)}, u32[]{:S(2)}) collective-permute-start(bf16[256,512]{1,0:T(8,128)(2,1)S(1)} %collective-permute-done.10.refs_5_), channel_id=1, source_target_pairs={{0,1},{1,0},{2,3},{3,2},{4,5},{5,4},{6,7},{7,6},{8,9},{9,8},{10,11... | collective-permute-start | bytes 786440 | tf_op jit(solution)/shard_map/ppermute | solution.py:14
  46.0 1.5 %collective-permute-start.13 = (bf16[256,512]{1,0:T(8,128)(2,1)S(1)}, bf16[256,512]{1,0:T(8,128)(2,1)S(1)}, u32[]{:S(2)}, u32[]{:S(2)}) collective-permute-start(bf16[256,512]{1,0:T(8,128)(2,1)S(1)} %collective-permute-done.12.refs_7_), channel_id=1, source_target_pairs={{0,1},{1,0},{2,3},{3,2},{4,5},{5,4},{6,7},{7,6},{8,9},{9,8},{10,11... | collective-permute-start | bytes 786440 | tf_op jit(solution)/shard_map/ppermute | solution.py:14
  46.0 1.8 %collective-permute-start.9 = (bf16[256,512]{1,0:T(8,128)(2,1)S(1)}, bf16[256,512]{1,0:T(8,128)(2,1)S(1)}, u32[]{:S(2)}, u32[]{:S(2)}) collective-permute-start(bf16[256,512]{1,0:T(8,128)(2,1)S(1)} %collective-permute-done.8.refs_3_), channel_id=1, source_target_pairs={{0,1},{1,0},{2,3},{3,2},{4,5},{5,4},{6,7},{7,6},{8,9},{9,8},{10,11... | collective-permute-start | bytes 786440 | tf_op jit(solution)/shard_map/ppermute | solution.py:14
  51.0 9.2 %collective-permute-start.14 = (bf16[256,512]{1,0:T(8,128)(2,1)S(1)}, bf16[256,512]{1,0:T(8,128)(2,1)S(1)}, u32[]{:S(2)}, u32[]{:S(2)}) collective-permute-start(bf16[256,512]{1,0:T(8,128)(2,1)S(1)} %get-tuple-element.26), channel_id=1, source_target_pairs={{0,8},{8,0},{16,24},{24,16},{1,9},{9,1},{17,25},{25,17},{2,10},{10... | collective-permute-start | bytes 786440 | tf_op jit(solution)/shard_map/ppermute | solution.py:14
  52.3 12.1 %collective-permute-start.15 = (bf16[256,512]{1,0:T(8,128)(2,1)S(1)}, bf16[256,512]{1,0:T(8,128)(2,1)S(1)}, u32[]{:S(2)}, u32[]{:S(2)}) collective-permute-start(bf16[256,512]{1,0:T(8,128)(2,1)S(1)} %get-tuple-element.27), channel_id=1, source_target_pairs={{0,16},{8,24},{16,0},{24,8},{1,17},{9,25},{17,1},{25,9},{2,18},{10... | collective-permute-start | bytes 786440 | tf_op jit(solution)/shard_map/ppermute | solution.py:14
  53.1 12.9 %collective-permute-start.16 = (bf16[256,512]{1,0:T(8,128)(2,1)S(1)}, bf16[256,512]{1,0:T(8,128)(2,1)S(1)}, u32[]{:S(2)}, u32[]{:S(2)}) collective-permute-start(bf16[256,512]{1,0:T(8,128)(2,1)S(1)} %get-tuple-element.28), channel_id=1, source_target_pairs={{0,24},{8,16},{16,8},{24,0},{1,25},{9,17},{17,9},{25,1},{2,26},{10... | collective-permute-start | bytes 786440 | tf_op jit(solution)/shard_map/ppermute | solution.py:14
  57.4 9.5 %collective-permute-start.4 = (bf16[256,512]{1,0:T(8,128)(2,1)}, bf16[256,512]{1,0:T(8,128)(2,1)S(1)}, u32[]{:S(2)}, u32[]{:S(2)}) collective-permute-start(bf16[256,512]{1,0:T(8,128)(2,1)} %get-tuple-element.20), channel_id=1, source_target_pairs={{0,2},{1,3},{2,0},{3,1},{4,6},{5,7},{6,4},{7,5},{8,10},{9,11},{10,... | collective-permute-start | bytes 786440 | tf_op jit(solution)/shard_map/ppermute | solution.py:14
  57.4 19.3 %collective-permute-start.5 = (bf16[256,512]{1,0:T(8,128)(2,1)}, bf16[256,512]{1,0:T(8,128)(2,1)S(1)}, u32[]{:S(2)}, u32[]{:S(2)}) collective-permute-start(bf16[256,512]{1,0:T(8,128)(2,1)} %get-tuple-element.21), channel_id=1, source_target_pairs={{0,4},{1,5},{2,6},{3,7},{4,0},{5,1},{6,2},{7,3},{8,12},{9,13},{10,... | collective-permute-start | bytes 786440 | tf_op jit(solution)/shard_map/ppermute | solution.py:14
  60.2 23.0 %collective-permute-start.6 = (bf16[256,512]{1,0:T(8,128)(2,1)}, bf16[256,512]{1,0:T(8,128)(2,1)S(1)}, u32[]{:S(2)}, u32[]{:S(2)}) collective-permute-start(bf16[256,512]{1,0:T(8,128)(2,1)} %get-tuple-element.22), channel_id=1, source_target_pairs={{0,6},{1,7},{2,4},{3,5},{4,2},{5,3},{6,0},{7,1},{8,14},{9,15},{10,... | collective-permute-start | bytes 786440 | tf_op jit(solution)/shard_map/ppermute | solution.py:14
